TPU v7x, 512 devices: a whole 4x8x8 slice. The times are simulated.
512 devices in a mesh: seq: 32 (over x_lo, y, core), head: 16 (over z, x_hi).
Axes of the slice: x: 4 (x_hi: 2, x_lo: 2; x = x_hi * 2 + x_lo), y: 8, z: 8, core: 2. Of those that a mesh axis runs over, the one named last changes fastest.
Arguments:
- queries: bfloat16 [32768, 4096], P(('seq', 'head')), may hold values from -200 to 200
- keys: bfloat16 [32768, 2048], P(('seq', 'head')), may hold values from -6.5 to 6.5
- values: bfloat16 [32768, 2048], P(('seq', 'head')), may hold values from -6 to 6
- visible: int32 [32, 4], P('seq'), may hold values 0 or 1
Outputs:
- attended: bfloat16 [32768, 4096], P(('seq', 'head'))
All inputs are finite; a program needn't handle non-finite values. No bound on the sum of `visible` on one device may be relied on, other than what follows from the above.
Results may differ from a plain program's by a relative error of at most 0.0045.
Values may be sent and summed in bfloat16 or wider, within the bound.
A program may use at most 128 MiB of HBM per device.

v0:
```python
import jax
import jax.numpy as jnp
from jax import lax
from jax.sharding import PartitionSpec as P

HEAD_SIZE = 128
QUERY_PER_KV = 2


attn_scale = 168.0 ** (-0.5)
powers = (1, 2, 4, 8)


def from_behind(shard, axis, by):
    count = lax.axis_size(axis)
    pairs = [(i, i + by) for i in range(count) if 0 <= i + by < count]
    return lax.ppermute(shard, axis, pairs)


def body(queries, keys, values, visible):
    keys_loc, values_loc = (
        lax.all_to_all(keys, "head", split_axis=1, concat_axis=0, tiled=True),
        lax.all_to_all(values, "head", split_axis=1, concat_axis=0, tiled=True),
    )
    query_loc = lax.all_to_all(queries, "head", split_axis=1, concat_axis=0, tiled=True)
    block_length = query_loc.shape[0]
    current = from_behind((keys_loc, values_loc), "seq", 1)
    remote = [current]
    for distance in (1, 2, 4):
        current = from_behind((current[0], current[1]), "seq", distance)
        remote.append(current)
    all_keys = jnp.concatenate([keys_loc] + [pair[0] for pair in remote], axis=0)
    all_values = jnp.concatenate([values_loc] + [pair[1] for pair in remote], axis=0)
    seq_index = lax.axis_index("seq")
    flag_arr = (visible[0] != 0) & (seq_index >= jnp.array(powers, jnp.int32))
    row_index = jnp.arange(block_length)[:, None]
    column = jnp.arange(5 * block_length)[None, :]
    region = column // block_length
    remote_ok = jnp.any(
        (region[None] == (jnp.arange(4) + 1)[:, None, None]) & flag_arr[:, None, None], axis=0
    )
    allowed = jnp.where(region == 0, column <= row_index, remote_ok)
    query_heads = query_loc.reshape(block_length, QUERY_PER_KV, HEAD_SIZE)
    outputs = []
    for member in range(QUERY_PER_KV):
        scores = (
            jnp.einsum(
                "qd,kd->qk", query_heads[:, member, :], all_keys, preferred_element_type=jnp.float32
            )
            * attn_scale
        )
        masked = jnp.where(allowed, scores, -1e30)
        peak = jnp.max(masked, axis=-1, keepdims=True)
        weights = jnp.where(allowed, jnp.exp(masked - peak), 0.0)
        total = jnp.sum(weights, axis=-1)
        rounded = weights.astype(jnp.bfloat16)
        numer = jnp.dot(rounded, all_values, preferred_element_type=jnp.float32)
        outputs.append((numer / total[:, None]).astype(jnp.bfloat16))
    merged = jnp.stack(outputs, axis=1).reshape(block_length, QUERY_PER_KV * HEAD_SIZE)
    return lax.all_to_all(merged, "head", split_axis=0, concat_axis=1, tiled=True)


def solution(mesh):
    return jax.shard_map(
        body,
        mesh=mesh,
        in_specs=(
            P(("seq", "head"), None),
            P(("seq", "head"), None),
            P(("seq", "head"), None),
            P("seq", None),
        ),
        out_specs=P(("seq", "head"), None),
        check_vma=False,
    )
```

profile of v0, /device:TPU:6, one launch (start us, length us, event | category | flops | bytes accessed | tf_op | source)
XLA Modules:
  0.0 182.2 jit_solution(17340840776345202195)
XLA Ops:
  0.0 0.9 copy-done
  1.7 13.3 %all-to-all-start = ((bf16[64,16,128]{2,0,1:T(8,128)(2,1)}), bf16[64,16,128]{2,0,1:T(8,128)(2,1)S(1)}, u32[]{:S(2)}, u32[]{:S(2)}) async-start(bf16[64,16,128]{2,0,1:T(8,128)(2,1)} %copy_bitcast_fusion.2), calls=%async_computation | async-start | bytes 524288 | tf_op jit(solution)/shard_map/all_to_all | solution.py:22
  15.0 1.7 copy_bitcast_fusion.1
  16.7 8.9 %all-to-all-done = bf16[64,16,128]{2,0,1:T(8,128)(2,1)S(1)} async-done(((bf16[64,16,128]{2,0,1:T(8,128)(2,1)}), bf16[64,16,128]{2,0,1:T(8,128)(2,1)S(1)}, u32[]{:S(2)}, u32[]{:S(2)}) %all-to-all-start) | async-done | bytes 262176 | tf_op jit(solution)/shard_map/all_to_all | solution.py:22
  25.6 6.4 %all-to-all-start.2 = ((bf16[64,16,128]{2,0,1:T(8,128)(2,1)}), bf16[64,16,128]{2,0,1:T(8,128)(2,1)S(1)}, u32[]{:S(2)}, u32[]{:S(2)}) async-start(bf16[64,16,128]{2,0,1:T(8,128)(2,1)} %copy_bitcast_fusion.1), calls=%async_computation.2 | async-start | bytes 524288 | tf_op jit(solution)/shard_map/all_to_all | solution.py:23
  32.0 1.9 %copy.42 = bf16[8,16,8,256]{3,2,0,1:T(8,128)(2,1)} copy(bf16[8,16,8,256]{3,2,1,0:T(8,128)(2,1)} %bitcast.70) | data formatting | bytes 1048576 | tf_op jit(solution)/shard_map/all_to_all | solution.py:25
  33.9 7.5 %all-to-all-done.2 = bf16[64,16,128]{2,0,1:T(8,128)(2,1)S(1)} async-done(((bf16[64,16,128]{2,0,1:T(8,128)(2,1)}), bf16[64,16,128]{2,0,1:T(8,128)(2,1)S(1)}, u32[]{:S(2)}, u32[]{:S(2)}) %all-to-all-start.2) | async-done | bytes 262176 | tf_op jit(solution)/shard_map/all_to_all | solution.py:23
  41.4 6.5 %all-to-all-start.1 = ((bf16[64,16,256]{2,0,1:T(8,128)(2,1)}), bf16[64,16,256]{2,0,1:T(8,128)(2,1)S(1)}, u32[]{:S(2)}, u32[]{:S(2)}) async-start(bf16[64,16,256]{2,0,1:T(8,128)(2,1)} %bitcast.63), calls=%async_computation.1 | async-start | bytes 1048576 | tf_op jit(solution)/shard_map/all_to_all | solution.py:25
  48.6 1.9 %collective-permute-start = (bf16[1024,128]{1,0:T(8,128)(2,1)S(1)}, bf16[1024,128]{1,0:T(8,128)(2,1)S(1)}, u32[]{:S(2)}, u32[]{:S(2)}) collective-permute-start(bf16[1024,128]{1,0:T(8,128)(2,1)S(1)} %bitcast.68), channel_id=1, source_target_pairs={{0,16},{16,32},{32,48},{48,64},{64,80},{80,96},{96,112},{112,128},... | collective-permute-start | bytes 786440 | tf_op jit(solution)/shard_map/ppermute | solution.py:17
  50.5 3.6 %collective-permute-start.4 = (bf16[1024,128]{1,0:T(8,128)(2,1)S(1)}, bf16[1024,128]{1,0:T(8,128)(2,1)S(1)}, u32[]{:S(2)}, u32[]{:S(2)}) collective-permute-start(bf16[1024,128]{1,0:T(8,128)(2,1)S(1)} %bitcast.66), channel_id=1, source_target_pairs={{0,16},{16,32},{32,48},{48,64},{64,80},{80,96},{96,112},{112,128},... | collective-permute-start | bytes 786440 | tf_op jit(solution)/shard_map/ppermute | solution.py:17
  54.3 6.0 %collective-permute-done = bf16[1024,128]{1,0:T(8,128)(2,1)S(1)} collective-permute-done((bf16[1024,128]{1,0:T(8,128)(2,1)S(1)}, bf16[1024,128]{1,0:T(8,128)(2,1)S(1)}, u32[]{:S(2)}, u32[]{:S(2)}) %collective-permute-start) | collective-permute-done | bytes 262176 | tf_op jit(solution)/shard_map/ppermute | solution.py:17
  60.3 1.9 %collective-permute-start.1 = (bf16[1024,128]{1,0:T(8,128)(2,1)S(1)}, bf16[1024,128]{1,0:T(8,128)(2,1)}, u32[]{:S(2)}, u32[]{:S(2)}) collective-permute-start(bf16[1024,128]{1,0:T(8,128)(2,1)S(1)} %collective-permute-done), channel_id=1, source_target_pairs={{0,16},{16,32},{32,48},{48,64},{64,80},{80,96},{96,112},{112,128},... | collective-permute-start | bytes 786440 | tf_op jit(solution)/shard_map/ppermute | solution.py:17
  62.2 1.5 collective-permute-done.4
  63.7 1.9 %collective-permute-start.5 = (bf16[1024,128]{1,0:T(8,128)(2,1)S(1)}, bf16[1024,128]{1,0:T(8,128)(2,1)}, u32[]{:S(2)}, u32[]{:S(2)}) collective-permute-start(bf16[1024,128]{1,0:T(8,128)(2,1)S(1)} %collective-permute-done.4), channel_id=1, source_target_pairs={{0,16},{16,32},{32,48},{48,64},{64,80},{80,96},{96,112},{112,128},... | collective-permute-start | bytes 786440 | tf_op jit(solution)/shard_map/ppermute | solution.py:17
  67.2 3.0 %collective-permute-done.1 = bf16[1024,128]{1,0:T(8,128)(2,1)} collective-permute-done((bf16[1024,128]{1,0:T(8,128)(2,1)S(1)}, bf16[1024,128]{1,0:T(8,128)(2,1)}, u32[]{:S(2)}, u32[]{:S(2)}) %collective-permute-start.1) | collective-permute-done | bytes 262176 | tf_op jit(solution)/shard_map/ppermute | solution.py:17
  70.2 1.9 %collective-permute-start.2 = (bf16[1024,128]{1,0:T(8,128)(2,1)}, bf16[1024,128]{1,0:T(8,128)(2,1)S(1)}, u32[]{:S(2)}, u32[]{:S(2)}) collective-permute-start(bf16[1024,128]{1,0:T(8,128)(2,1)} %collective-permute-done.1), channel_id=1, source_target_pairs={{0,32},{16,48},{32,64},{48,80},{64,96},{80,112},{96,128},{112,144}... | collective-permute-start | bytes 786440 | tf_op jit(solution)/shard_map/ppermute | solution.py:17
  72.1 1.5 collective-permute-done.5
  73.6 1.9 %collective-permute-start.6 = (bf16[1024,128]{1,0:T(8,128)(2,1)}, bf16[1024,128]{1,0:T(8,128)(2,1)S(1)}, u32[]{:S(2)}, u32[]{:S(2)}) collective-permute-start(bf16[1024,128]{1,0:T(8,128)(2,1)} %collective-permute-done.5), channel_id=1, source_target_pairs={{0,32},{16,48},{32,64},{48,80},{64,96},{80,112},{96,128},{112,144}... | collective-permute-start | bytes 786440 | tf_op jit(solution)/shard_map/ppermute | solution.py:17
  76.2 1.0 constant_dynamic-update-slice_fusion.2
  77.2 5.6 %collective-permute-done.2 = bf16[1024,128]{1,0:T(8,128)(2,1)S(1)} collective-permute-done((bf16[1024,128]{1,0:T(8,128)(2,1)}, bf16[1024,128]{1,0:T(8,128)(2,1)S(1)}, u32[]{:S(2)}, u32[]{:S(2)}) %collective-permute-start.2) | collective-permute-done | bytes 262176 | tf_op jit(solution)/shard_map/ppermute | solution.py:17
  82.8 1.9 %collective-permute-start.3 = (bf16[1024,128]{1,0:T(8,128)(2,1)S(1)}, bf16[1024,128]{1,0:T(8,128)(2,1)S(1)}, u32[]{:S(2)}, u32[]{:S(2)}) collective-permute-start(bf16[1024,128]{1,0:T(8,128)(2,1)S(1)} %collective-permute-done.2), channel_id=1, source_target_pairs={{0,64},{16,80},{32,96},{48,112},{64,128},{80,144},{96,160},{112,17... | collective-permute-start | bytes 786440 | tf_op jit(solution)/shard_map/ppermute | solution.py:17
  84.8 1.7 constant_dynamic-update-slice_fusion.7
  86.4 1.7 collective-permute-done.6
  88.1 2.4 %collective-permute-start.7 = (bf16[1024,128]{1,0:T(8,128)(2,1)S(1)}, bf16[1024,128]{1,0:T(8,128)(2,1)}, u32[]{:S(2)}, u32[]{:S(2)}) collective-permute-start(bf16[1024,128]{1,0:T(8,128)(2,1)S(1)} %collective-permute-done.6), channel_id=1, source_target_pairs={{0,64},{16,80},{32,96},{48,112},{64,128},{80,144},{96,160},{112,17... | collective-permute-start | bytes 786440 | tf_op jit(solution)/shard_map/ppermute | solution.py:17
  91.2 9.2 %collective-permute-done.3 = bf16[1024,128]{1,0:T(8,128)(2,1)S(1)} collective-permute-done((bf16[1024,128]{1,0:T(8,128)(2,1)S(1)}, bf16[1024,128]{1,0:T(8,128)(2,1)S(1)}, u32[]{:S(2)}, u32[]{:S(2)}) %collective-permute-start.3) | collective-permute-done | bytes 262176 | tf_op jit(solution)/shard_map/ppermute | solution.py:17
  100.5 2.9 %fusion.25 = f32[5120,1024]{1,0:T(8,128)S(1)} fusion(bf16[5120,128]{1,0:T(8,128)(2,1)S(1)} %constant_dynamic-update-slice_fusion, bf16[1024,1,128]{2,1,0:T(2,128)(2,1)S(1)} %get-tuple-element.9), kind=kOutput, calls=%fused_computation.22 | convolution fusion | flops 1342177280 | bytes 22544384 | tf_op jit(solution)/shard_map/qd,kd->qk/dot_general | solution.py:47
  103.4 12.4 %fusion.1 = (f32[1024]{0:T(1024)S(1)}, f32[1024]{0:T(1024)S(1)}, f32[5120,1024]{1,0:T(8,128)}) fusion(pred[5120]{0:T(1024)(128)(4,1)S(1)} %and_reduce_fusion, pred[5120]{0:T(1024)(128)(4,1)S(1)} %broadcast_compare_fusion, f32[5120,1024]{1,0:T(8,128)S(1)} %fusion.25, bf16[5120,128]{1,0:T(8,128)(2,1)S(1)} %constant_dynamic-update-slice_fusion, ...), kind=kOutput, calls=%fused_computation.6 | convolution fusion | flops 1384118272 | bytes 43534336 | tf_op jit(solution)/shard_map/qd,kd->qk/dot_general | solution.py:47
  115.9 19.1 %fusion.34 = (f32[1024]{0:T(1024)S(1)}, f32[1024]{0:T(1024)S(1)}) fusion(f32[1024]{0:T(1024)S(1)} %get-tuple-element.7, f32[5120,1024]{1,0:T(8,128)} %get-tuple-element.11, pred[5120]{0:T(1024)(128)(4,1)S(1)} %and_reduce_fusion, pred[5120]{0:T(1024)(128)(4,1)S(1)} %broadcast_compare_fusion, f32[1024]{0:T(1024)S(1)} %get-tuple-element.8, ...), kind=kLoop, calls=%fused_computation.49 | loop fusion | flops 62912512 | bytes 41969664 | tf_op jit(solution)/shard_map/reduce_sum | solution.py:55
  134.9 1.7 constant_dynamic-update-slice_fusion.5
  136.6 13.3 %fusion.13 = bf16[1024,1,128]{2,0,1:T(8,128)(2,1)S(1)} fusion(bf16[5120,128]{1,0:T(8,128)(2,1)} %constant_dynamic-update-slice_fusion.5, f32[1024]{0:T(1024)S(1)} %get-tuple-element.5, f32[5120,1024]{1,0:T(8,128)} %get-tuple-element.11, f32[1024]{0:T(1024)S(1)} %get-tuple-element.7, pred[5120]{0:T(1024)(128)(4,1)S(1)} %and_reduce_fusion, ...), kind=kOutput, calls=%fused_computation.14 | convolution fusion | flops 1379139584 | bytes 22562816 | tf_op jit(solution)/shard_map/dot_general | solution.py:57
  149.9 8.3 %fusion.22 = bf16[1024,1,128]{2,0,1:T(8,128)(2,1)S(1)} fusion(bf16[5120,128]{1,0:T(8,128)(2,1)} %constant_dynamic-update-slice_fusion.5, f32[1024]{0:T(1024)S(1)} %get-tuple-element.6, f32[5120,1024]{1,0:T(8,128)S(1)} %fusion.25, f32[1024]{0:T(1024)S(1)} %get-tuple-element.8, pred[5120]{0:T(1024)(128)(4,1)S(1)} %and_reduce_fusion, ...), kind=kOutput, calls=%fused_computation.17 | convolution fusion | flops 1379139584 | bytes 22562816 | tf_op jit(solution)/shard_map/dot_general | solution.py:57
  159.2 22.2 %all_to_all.73 = bf16[16,64,256]{2,1,0:T(8,128)(2,1)S(1)} all-to-all(bf16[16,64,256]{2,1,0:T(8,128)(2,1)S(1)} %all_to_all.65), channel_id=1, replica_groups=mesh['seq'=32,'head'=16] {'head'}, dimensions={0} | all-to-all | bytes 1048576 | tf_op jit(solution)/shard_map/all_to_all | solution.py:60
  (22 shorter events, 6.5 us)
Async XLA Ops:
  0.0 1.0 copy-start
  1.7 23.9 %all-to-all-start = ((bf16[64,16,128]{2,0,1:T(8,128)(2,1)}), bf16[64,16,128]{2,0,1:T(8,128)(2,1)S(1)}, u32[]{:S(2)}, u32[]{:S(2)}) async-start(bf16[64,16,128]{2,0,1:T(8,128)(2,1)} %copy_bitcast_fusion.2), calls=%async_computation | async-start | bytes 524288 | tf_op jit(solution)/shard_map/all_to_all | solution.py:22
  25.6 15.8 %all-to-all-start.2 = ((bf16[64,16,128]{2,0,1:T(8,128)(2,1)}), bf16[64,16,128]{2,0,1:T(8,128)(2,1)S(1)}, u32[]{:S(2)}, u32[]{:S(2)}) async-start(bf16[64,16,128]{2,0,1:T(8,128)(2,1)} %copy_bitcast_fusion.1), calls=%async_computation.2 | async-start | bytes 524288 | tf_op jit(solution)/shard_map/all_to_all | solution.py:23
  41.4 25.7 %all-to-all-start.1 = ((bf16[64,16,256]{2,0,1:T(8,128)(2,1)}), bf16[64,16,256]{2,0,1:T(8,128)(2,1)S(1)}, u32[]{:S(2)}, u32[]{:S(2)}) async-start(bf16[64,16,256]{2,0,1:T(8,128)(2,1)} %bitcast.63), calls=%async_computation.1 | async-start | bytes 1048576 | tf_op jit(solution)/shard_map/all_to_all | solution.py:25
  48.6 11.7 %collective-permute-start = (bf16[1024,128]{1,0:T(8,128)(2,1)S(1)}, bf16[1024,128]{1,0:T(8,128)(2,1)S(1)}, u32[]{:S(2)}, u32[]{:S(2)}) collective-permute-start(bf16[1024,128]{1,0:T(8,128)(2,1)S(1)} %bitcast.68), channel_id=1, source_target_pairs={{0,16},{16,32},{32,48},{48,64},{64,80},{80,96},{96,112},{112,128},... | collective-permute-start | bytes 786440 | tf_op jit(solution)/shard_map/ppermute | solution.py:17
  50.5 13.1 %collective-permute-start.4 = (bf16[1024,128]{1,0:T(8,128)(2,1)S(1)}, bf16[1024,128]{1,0:T(8,128)(2,1)S(1)}, u32[]{:S(2)}, u32[]{:S(2)}) collective-permute-start(bf16[1024,128]{1,0:T(8,128)(2,1)S(1)} %bitcast.66), channel_id=1, source_target_pairs={{0,16},{16,32},{32,48},{48,64},{64,80},{80,96},{96,112},{112,128},... | collective-permute-start | bytes 786440 | tf_op jit(solution)/shard_map/ppermute | solution.py:17
  60.3 9.9 %collective-permute-start.1 = (bf16[1024,128]{1,0:T(8,128)(2,1)S(1)}, bf16[1024,128]{1,0:T(8,128)(2,1)}, u32[]{:S(2)}, u32[]{:S(2)}) collective-permute-start(bf16[1024,128]{1,0:T(8,128)(2,1)S(1)} %collective-permute-done), channel_id=1, source_target_pairs={{0,16},{16,32},{32,48},{48,64},{64,80},{80,96},{96,112},{112,128},... | collective-permute-start | bytes 786440 | tf_op jit(solution)/shard_map/ppermute | solution.py:17
  63.7 9.9 %collective-permute-start.5 = (bf16[1024,128]{1,0:T(8,128)(2,1)S(1)}, bf16[1024,128]{1,0:T(8,128)(2,1)}, u32[]{:S(2)}, u32[]{:S(2)}) collective-permute-start(bf16[1024,128]{1,0:T(8,128)(2,1)S(1)} %collective-permute-done.4), channel_id=1, source_target_pairs={{0,16},{16,32},{32,48},{48,64},{64,80},{80,96},{96,112},{112,128},... | collective-permute-start | bytes 786440 | tf_op jit(solution)/shard_map/ppermute | solution.py:17
  70.2 12.7 %collective-permute-start.2 = (bf16[1024,128]{1,0:T(8,128)(2,1)}, bf16[1024,128]{1,0:T(8,128)(2,1)S(1)}, u32[]{:S(2)}, u32[]{:S(2)}) collective-permute-start(bf16[1024,128]{1,0:T(8,128)(2,1)} %collective-permute-done.1), channel_id=1, source_target_pairs={{0,32},{16,48},{32,64},{48,80},{64,96},{80,112},{96,128},{112,144}... | collective-permute-start | bytes 786440 | tf_op jit(solution)/shard_map/ppermute | solution.py:17
  73.6 14.5 %collective-permute-start.6 = (bf16[1024,128]{1,0:T(8,128)(2,1)}, bf16[1024,128]{1,0:T(8,128)(2,1)S(1)}, u32[]{:S(2)}, u32[]{:S(2)}) collective-permute-start(bf16[1024,128]{1,0:T(8,128)(2,1)} %collective-permute-done.5), channel_id=1, source_target_pairs={{0,32},{16,48},{32,64},{48,80},{64,96},{80,112},{96,128},{112,144}... | collective-permute-start | bytes 786440 | tf_op jit(solution)/shard_map/ppermute | solution.py:17
  82.8 17.6 %collective-permute-start.3 = (bf16[1024,128]{1,0:T(8,128)(2,1)S(1)}, bf16[1024,128]{1,0:T(8,128)(2,1)S(1)}, u32[]{:S(2)}, u32[]{:S(2)}) collective-permute-start(bf16[1024,128]{1,0:T(8,128)(2,1)S(1)} %collective-permute-done.2), channel_id=1, source_target_pairs={{0,64},{16,80},{32,96},{48,112},{64,128},{80,144},{96,160},{112,17... | collective-permute-start | bytes 786440 | tf_op jit(solution)/shard_map/ppermute | solution.py:17
  88.1 46.8 %collective-permute-start.7 = (bf16[1024,128]{1,0:T(8,128)(2,1)S(1)}, bf16[1024,128]{1,0:T(8,128)(2,1)}, u32[]{:S(2)}, u32[]{:S(2)}) collective-permute-start(bf16[1024,128]{1,0:T(8,128)(2,1)S(1)} %collective-permute-done.6), channel_id=1, source_target_pairs={{0,64},{16,80},{32,96},{48,112},{64,128},{80,144},{96,160},{112,17... | collective-permute-start | bytes 786440 | tf_op jit(solution)/shard_map/ppermute | solution.py:17
where the time goes:
time: 186 us; the launch traced here: 182 us
  waiting for transfers between devices  44.8 us (24%)
  starting transfers between devices  43.6 us (23%)
  matrix products  37 us (20%)
  blocking collectives  22.2 us (12%)
  other arithmetic  19.9 us (11%)
  local copies, waits for them, and re-layouts  14.5 us (8%)
    ppermute x8, waiting for transfers between devices, from_behind(): return lax.ppermute(shard, axis, pairs)  28.4 us
    all_to_all x1, blocking collectives, body(): lax.all_to_all(merged, 'head', split_axis=0, concat_axis=1, tiled=True)  22.2 us
    dot_general x2, matrix products, body(): numer = jnp.dot(rounded, all_values, preferred_element_type=jnp.float32)  21.7 us
    reduce_sum x1, other arithmetic, body(): total = jnp.sum(weights, axis=-1)  19.1 us
    ppermute x8, starting transfers between devices, from_behind(): return lax.ppermute(shard, axis, pairs)  17.4 us
    dot_general x2, matrix products, body(): jnp.einsum('qd,kd->qk', query_heads[:, member, :], all_keys, preferred_el...  15.3 us
    all_to_all x1, starting transfers between devices, body(): lax.all_to_all(keys, 'head', split_axis=1, concat_axis=0, tiled=True)  13.3 us
    all_to_all x1, waiting for transfers between devices, body(): lax.all_to_all(keys, 'head', split_axis=1, concat_axis=0, tiled=True)  8.86 us
  transfers between devices with their start and end apart: 11, of which 9 were waited for; matrix products, arithmetic and copies ran while one was open for 24% of the time, Pallas kernels for 0%

commit v1 on v0

v1 whole, which is shorter than its diff:
```python
import functools

import jax
import jax.numpy as jnp
from jax import lax
from jax.experimental import pallas as pl
from jax.experimental.pallas import tpu as pltpu
from jax.sharding import PartitionSpec as P

D = 128
RUN = 128
NZ = 8
BLOCK = 1024
SCALE2 = 168.0 ** (-0.5) * 1.4426950408889634
NM = 5
HIDE = 1e30
MESH = pl.DeviceIdType.MESH
F32 = jnp.float32
BF16 = jnp.bfloat16


def offset(i):
    return jnp.where(i % 2 == 1, (i + 1) // 2, (NZ - i // 2) % NZ)


def kernel(vis_ref, q_ref, k_ref, v_ref, o_ref, qbuf, kv, relay, vx, obuf, acc, peak,
           s_a, s_b, p_a, p_b,
           kv0_sem, q_sem, kv_sem, rl_sem, o_sem, in_send, f1_send, f2_send, f3_send, f4_send,
           m_send, mr_send, o_send):
    s = lax.axis_index("seq")
    h = lax.axis_index("head")
    z, xh = h // 2, h % 2
    core, chip = s % 2, s // 2
    xl, y = chip // 8, chip % 8
    relay_to = (xl * 8 + (y + 6) % 8) * 2 + core
    relay_chip = xl * 8 + (y + 2) % 8
    relay_from = relay_chip * 2 + core
    relays = relay_chip < 12
    relay_dst = relay_from + 8
    src8 = s - 8
    chip8 = src8 // 2
    relay_src = ((chip8 // 8) * 8 + (chip8 % 8 + 6) % 8) * 2 + core

    bar = pltpu.get_barrier_semaphore()

    @pl.loop(1, 16)
    def _(n):
        pl.semaphore_signal(bar, inc=1, device_id={"head": (h + n) % 16}, device_id_type=MESH)

    links = [
        (True, s + 1 - 2 * core),
        (s + 2 < 32, s + 2), (s >= 2, s - 2),
        (s + 4 < 32, s + 4), (s >= 4, s - 4),
        (s + 8 < 32, relay_to), (relays, relay_from),
        (relays, relay_dst), (s >= 8, relay_src),
    ]
    count = 15
    for cond, other in links:
        if cond is True:
            pl.semaphore_signal(bar, inc=1, device_id={"seq": other}, device_id_type=MESH)
            count = count + 1
        else:
            @pl.when(cond)
            def _():
                pl.semaphore_signal(bar, inc=1, device_id={"seq": other}, device_id_type=MESH)
            count = count + cond.astype(jnp.int32)
    pl.semaphore_wait(bar, count)

    def rows64(x):
        return pl.ds(pl.multiple_of(x * 64, 64), 64)

    def cols(i, width):
        return pl.ds(pl.multiple_of(i * width, width), width)

    def pieces(p):
        yield k_ref.at[:, cols(p, D)], kv.at[0, z, 0, rows64(xh)], in_send.at[0], kv0_sem.at[z]
        yield v_ref.at[:, cols(p, D)], kv.at[0, z, 1, rows64(xh)], in_send.at[1], kv0_sem.at[z]

    def q_pieces(p):
        for g in range(2):
            yield q_ref.at[:, cols(p * 2 + g, D)], qbuf.at[z, g, rows64(xh)], in_send.at[2], q_sem.at[z]

    for src, dst, _, sem in pieces(h):
        pltpu.make_async_copy(src, dst, sem).start()
    for src, dst, _, sem in q_pieces(h):
        pltpu.make_async_copy(src, dst, sem).start()
    for each in (pieces, q_pieces):
        @pl.loop(1, 16)
        def _(n):
            p = ((z + offset(n // 2)) % NZ) * 2 + (xh + n) % 2
            for src, dst, send, recv in each(p):
                pltpu.make_async_remote_copy(src, dst, send, recv, device_id={"head": p}, device_id_type=MESH).start()

    def zof(i):
        return (z + offset(i)) % NZ

    def wait_bytes(ref, sem):
        pltpu.make_async_copy(ref, ref, sem).wait()

    def pass_on(src, dst, send, recv, to):
        pltpu.make_async_remote_copy(src, dst, send, recv, device_id={"seq": to}, device_id_type=MESH).start()

    def own(i):
        r = zof(i)
        wait_bytes(kv.at[0, r], kv0_sem.at[r])

        @pl.when(core == 0)
        def _():
            pass_on(kv.at[0, r], kv.at[1, r], f1_send, kv_sem.at[0, r], s + 1)

        @pl.when(s + 2 < 32)
        def _():
            pass_on(kv.at[0, r], kv.at[2, r], f2_send, kv_sem.at[1, r], s + 2)

        @pl.when((s + 8 < 32) & (i < NM))
        def _():
            pass_on(kv.at[0, r], relay.at[i], m_send, rl_sem.at[i], relay_to)

    def two_back(i):
        r = zof(i)

        @pl.when(s >= 2)
        def _():
            wait_bytes(kv.at[2, r], kv_sem.at[1, r])

        @pl.when((s >= 2) & (core == 1))
        def _():
            pass_on(kv.at[2, r], kv.at[1, r], f1_send, kv_sem.at[0, r], s - 1)

    def to_four(i):
        r = zof(i)

        @pl.when((s >= 2) & (s + 2 < 32))
        def _():
            pass_on(kv.at[2, r], kv.at[3, r], f3_send, kv_sem.at[2, r], s + 2)

    def four_back(i):
        r = zof(i)

        @pl.when(s >= 4)
        def _():
            wait_bytes(kv.at[3, r], kv_sem.at[2, r])

        @pl.when((s >= 4) & (s + 4 < 32) & (i >= NM))
        def _():
            pass_on(kv.at[3, r], kv.at[4, r], f4_send, kv_sem.at[3, r], s + 4)

    def relayed(i):
        r = zof(i)

        @pl.when(relays)
        def _():
            wait_bytes(relay.at[i], rl_sem.at[i])
            pass_on(relay.at[i], kv.at[4, r], mr_send, kv_sem.at[3, r], relay_dst)

    for j, dist in ((1, 1), (2, 2), (3, 4), (4, 8)):
        @pl.when(s < dist)
        def _():
            kv[j] = jnp.zeros(kv.shape[1:], BF16)
    for j in range(5):
        vx[j, :, D:] = jnp.ones((BLOCK, D), BF16)

    for k in range(NZ):
        own(k)
        if k >= 2:
            two_back(k - 2)
        if k in (3, 5, 7):
            relayed((k - 3) // 2)
    two_back(6)
    two_back(7)

    @pl.loop(0, NZ)
    def _(i):
        to_four(i)

    @pl.when(s >= 1)
    def _():
        @pl.loop(0, NZ)
        def _(i):
            wait_bytes(kv.at[1, i], kv_sem.at[0, i])

    for j in range(3):
        vx[j, :, :D] = kv[j, :, 1].reshape(BLOCK, D)

    flags = [(vis_ref[0, j] != 0) & (s >= 2 ** j) for j in range(4)]
    dims = (((1,), (1,)), ((), ()))

    def scores3(i, buf):
        r = zof(i)
        wait_bytes(qbuf.at[r], q_sem.at[r])
        q = qbuf[r].reshape(2 * RUN, D)
        for j in range(3):
            buf[:, j * BLOCK:(j + 1) * BLOCK] = lax.dot_general(
                q, kv[j, :, 0].reshape(BLOCK, D), dims, preferred_element_type=F32)

    row = lax.broadcasted_iota(jnp.int32, (2 * RUN, BLOCK), 0) % RUN
    column = lax.broadcasted_iota(jnp.int32, (2 * RUN, BLOCK), 1)
    ahead = column - row

    def soft3(i, buf, out):
        r = zof(i)
        s0 = jnp.where(ahead <= r * RUN, buf[:, :BLOCK], -HIDE)
        s1, s2 = buf[:, BLOCK:2 * BLOCK], buf[:, 2 * BLOCK:]
        top = jnp.max(s0, axis=1, keepdims=True)
        for part, flag in ((s1, flags[0]), (s2, flags[1])):
            here = jnp.max(part, axis=1, keepdims=True)
            top = jnp.where(flag, jnp.maximum(top, here), top)
        low = top * SCALE2
        peak[r] = jnp.broadcast_to(low, (2 * RUN, D))
        out[:, :BLOCK] = jnp.exp2(s0 * SCALE2 - low).astype(BF16)
        for n, (part, flag) in enumerate(((s1, flags[0]), (s2, flags[1]))):
            out[:, (n + 1) * BLOCK:(n + 2) * BLOCK] = jnp.exp2(
                part * SCALE2 - jnp.where(flag, low, HIDE)).astype(BF16)

    def value3(i, out):
        acc[zof(i)] = jnp.dot(out[...], vx[0:3].reshape(3 * BLOCK, 2 * D), preferred_element_type=F32)

    scores3(0, s_a)
    scores3(1, s_b)
    soft3(0, s_a, p_a)

    @pl.loop(0, 3)
    def _(n):
        i = 2 * n

        relayed_if(relayed, n + 3)
        value3(i, p_a)
        scores3(i + 2, s_a)
        soft3(i + 1, s_b, p_b)
        value3(i + 1, p_b)
        scores3(i + 3, s_b)
        soft3(i + 2, s_a, p_a)

    value3(6, p_a)
    soft3(7, s_b, p_b)
    value3(7, p_b)

    @pl.loop(0, NZ)
    def _(i):
        four_back(i)

    def scores1(j, i, buf):
        buf[:, :BLOCK] = lax.dot_general(
            qbuf[zof(i)].reshape(2 * RUN, D), kv[j, :, 0].reshape(BLOCK, D), dims, preferred_element_type=F32)

    def soft1(j, i, buf, out):
        r = zof(i)
        flag = flags[j - 1]
        part = buf[:, :BLOCK]
        old = peak[r, :, 0:1]
        low = jnp.where(flag, jnp.maximum(old, jnp.max(part, axis=1, keepdims=True) * SCALE2), old)
        peak[r] = jnp.broadcast_to(low, (2 * RUN, D))
        acc[r] = acc[r] * jnp.exp2(old - low)
        out[:, :BLOCK] = jnp.exp2(part * SCALE2 - jnp.where(flag, low, HIDE)).astype(BF16)

    def value1(j, i, out):
        r = zof(i)
        total = acc[r] + jnp.dot(out[:, :BLOCK], vx[j], preferred_element_type=F32)
        if j < 4:
            acc[r] = total
            return
        done = (total[:, :D] / total[:, D:]).astype(BF16)
        obuf[r, :, :D] = done[:RUN]
        obuf[r, :, D:] = done[RUN:]
        for x in range(2):
            p = r * 2 + x
            src, dst = obuf.at[r, x * 64:(x + 1) * 64], o_ref.at[:, cols(h, 2 * D)]

            @pl.when(p == h)
            def _():
                pltpu.make_async_copy(src, dst, o_sem).start()

            @pl.when(p != h)
            def _():
                pltpu.make_async_remote_copy(src, dst, o_send, o_sem, device_id={"head": p}, device_id_type=MESH).start()

    def block(j):
        vx[j, :, :D] = kv[j, :, 1].reshape(BLOCK, D)
        scores1(j, 7, s_a)
        scores1(j, 6, s_b)
        soft1(j, 7, s_a, p_a)

        @pl.loop(0, 3)
        def _(n):
            i = 7 - 2 * n
            value1(j, i, p_a)
            scores1(j, i - 2, s_a)
            soft1(j, i - 1, s_b, p_b)
            value1(j, i - 1, p_b)
            scores1(j, i - 3, s_b)
            soft1(j, i - 2, s_a, p_a)

        value1(j, 1, p_a)
        soft1(j, 0, s_b, p_b)
        value1(j, 0, p_b)

    block(3)

    @pl.when(s >= 8)
    def _():
        @pl.loop(0, NZ)
        def _(i):
            wait_bytes(kv.at[4, i], kv_sem.at[3, i])

    block(4)

    wait_bytes(k_ref.at[:, :15 * D], in_send.at[0])
    wait_bytes(v_ref.at[:, :15 * D], in_send.at[1])
    wait_bytes(q_ref.at[:, :30 * D], in_send.at[2])
    whole = kv.at[0]
    for cond, ref, sem in (
        ((core == 0) | (s >= 2), whole, f1_send),
        (s + 2 < 32, whole, f2_send),
        ((s >= 2) & (s + 2 < 32), whole, f3_send),
        ((s >= 4) & (s + 4 < 32), kv.at[0, 0:NZ - NM], f4_send),
        (s + 8 < 32, kv.at[0, 0:NM], m_send),
        (relays, kv.at[0, 0:NM], mr_send),
    ):
        @pl.when(cond)
        def _():
            wait_bytes(ref, sem)
    wait_bytes(o_ref.at[:, :30 * D], o_send)
    wait_bytes(o_ref, o_sem)


def relayed_if(relayed, i):
    @pl.when(i < NM)
    def _():
        relayed(i)


def body(queries, keys, values, visible):
    dma = pltpu.SemaphoreType.DMA
    return pl.pallas_call(
        kernel,
        out_shape=jax.ShapeDtypeStruct(queries.shape, BF16),
        in_specs=[pl.BlockSpec(memory_space=pltpu.SMEM)] + [pl.BlockSpec(memory_space=pl.ANY)] * 3,
        out_specs=pl.BlockSpec(memory_space=pl.ANY),
        scratch_shapes=[
            pltpu.VMEM((NZ, 2, RUN, D), BF16),
            pltpu.VMEM((5, NZ, 2, RUN, D), BF16),
            pltpu.VMEM((NM, 2, RUN, D), BF16),
            pltpu.VMEM((5, BLOCK, 2 * D), BF16),
            pltpu.VMEM((NZ, RUN, 2 * D), BF16),
            pltpu.VMEM((NZ, 2 * RUN, 2 * D), F32),
            pltpu.VMEM((NZ, 2 * RUN, D), F32),
            pltpu.VMEM((2 * RUN, 3 * BLOCK), F32),
            pltpu.VMEM((2 * RUN, 3 * BLOCK), F32),
            pltpu.VMEM((2 * RUN, 3 * BLOCK), BF16),
            pltpu.VMEM((2 * RUN, 3 * BLOCK), BF16),
            dma((NZ,)), dma((NZ,)), dma((4, NZ)), dma((NM,)), dma,
            dma((3,)), dma, dma, dma, dma, dma, dma, dma,
        ],
        compiler_params=pltpu.CompilerParams(
            collective_id=0, has_side_effects=True, vmem_limit_bytes=56 * 2**20),
        cost_estimate=pl.CostEstimate(flops=5 * 10**9, bytes_accessed=2 * 10**6, transcendentals=10**7),
    )(visible, queries, keys, values)


def solution(mesh):
    rows = P(("seq", "head"), None)
    return jax.shard_map(
        body,
        mesh=mesh,
        in_specs=(rows, rows, rows, P("seq", None)),
        out_specs=rows,
        check_vma=False,
    )
```

time: 186 us -> 82.3 us (0.44); the launches traced: 182 us -> 82.1 us
  Pallas kernels: 0 us -> 80.3 us
  waiting for transfers between devices: 44.8 us -> 0 us
  starting transfers between devices: 43.6 us -> 0 us
  matrix products: 37 us -> 0 us
  blocking collectives: 22.2 us -> 0 us
  other arithmetic: 19.9 us -> 0 us
  local copies, waits for them, and re-layouts: 14.5 us -> 1.87 us
    pallas_call x0 -> x1, Pallas kernels: none -> 80.3 us  [body(): pl.pallas_call(kernel, out_shape=jax.ShapeDtypeStruct(queries.shape, BF16...]
    dot_general x4 -> x0, matrix products: 37 us -> none  [the longest x2 21.7 us: body(): numer = jnp.dot(rounded, all_values, preferred_element_type=jnp.float32)]
    ppermute x8 -> x0, waiting for transfers between devices: 28.4 us -> none  [from_behind(): return lax.ppermute(shard, axis, pairs)]
    all_to_all x3 -> x0, starting transfers between devices: 26.2 us -> none  [the longest x1 13.3 us: body(): lax.all_to_all(keys, 'head', split_axis=1, concat_axis=0, tiled=True)]
    all_to_all x1 -> x0, blocking collectives: 22.2 us -> none  [body(): lax.all_to_all(merged, 'head', split_axis=0, concat_axis=1, tiled=True)]
    reduce_sum x1 -> x0, other arithmetic: 19.1 us -> none  [body(): total = jnp.sum(weights, axis=-1)]
    ppermute x8 -> x0, starting transfers between devices: 17.4 us -> none  [from_behind(): return lax.ppermute(shard, axis, pairs)]
    all_to_all x3 -> x0, waiting for transfers between devices: 16.4 us -> none  [the longest x1 8.86 us: body(): lax.all_to_all(keys, 'head', split_axis=1, concat_axis=0, tiled=True)]
  transfers between devices with their start and end apart: 11 -> 0, of which waited for: 9 -> 0; matrix products, arithmetic and copies ran while one was open for 24% -> 0% of each run, Pallas kernels for 0% -> 0%
where the time goes in v1:
time: 82.3 us; the launch traced here: 82.1 us
  Pallas kernels  80.3 us (98%)
  local copies, waits for them, and re-layouts  1.87 us (2%)
    pallas_call x1, Pallas kernels, body(): pl.pallas_call(kernel, out_shape=jax.ShapeDtypeStruct(queries.shape, BF16...  80.3 us
    unnamed x1, local copies, waits for them, and re-layouts  1.87 us

profile of v1, /device:TPU:6, one launch (start us, length us, event | category | flops | bytes accessed | tf_op | source)
XLA Modules:
  0.0 82.1 jit_solution(5116592206705814648)
XLA Ops:
  0.0 80.3 %shard_map.46 = bf16[64,4096]{1,0:T(8,128)(2,1)} custom-call(s32[1,4]{1,0:T(1,128)} %vis_ref.1, bf16[64,4096]{1,0:T(8,128)(2,1)} %q_ref.1, bf16[64,2048]{1,0:T(8,128)(2,1)} %k_ref.1, bf16[64,2048]{1,0:T(8,128)(2,1)} %v_ref.1), custom_call_target="tpu_custom_call" | custom-call | flops 5000000000 | bytes 2000000 | tf_op jit(solution)/shard_map/pallas_call | solution.py:334
  80.3 1.9 %copy.6 = bf16[64,4096]{1,0:T(8,128)(2,1)} copy(bf16[64,4096]{1,0:T(8,128)(2,1)} %shard_map.46) | data formatting | bytes 1048576

commit v2 on v1

--- a/solution.py
+++ b/solution.py
@@ -12,8 +12,47 @@
 NZ = 8
 BLOCK = 1024
 SCALE2 = 168.0 ** (-0.5) * 1.4426950408889634
+AHEAD = 8
 NM = 5
 HIDE = 1e30
+PLAN = (
+    ("own", 0),
+    ("own", 1),
+    ("own", 2),
+    ("two", 0),
+    ("four", 0),
+    ("relay", 0),
+    ("own", 3),
+    ("own", 4),
+    ("two", 1),
+    ("four", 1),
+    ("two", 2),
+    ("four", 2),
+    ("relay", 1),
+    ("own", 5),
+    ("two", 3),
+    ("four", 3),
+    ("own", 6),
+    ("two", 4),
+    ("four", 4),
+    ("own", 7),
+    ("two", 5),
+    ("four", 5),
+    ("relay", 2),
+    ("two", 6),
+    ("four", 6),
+    ("two", 7),
+    ("four", 7),
+)
+LATER = (
+    (("cross", 0),),
+    (("cross", 1), ("relay", 3)),
+    (("cross", 2), ("cross", 3)),
+    (("cross", 4), ("relay", 4)),
+    (("cross", 5), ("old", 0), ("old", 1), ("old", 2), ("old", 3), ("old", 4), ("old", 5)),
+    (("cross", 6), ("old", 6)),
+    (("cross", 7), ("old", 7)),
+)
 MESH = pl.DeviceIdType.MESH
 F32 = jnp.float32
 BF16 = jnp.bfloat16
@@ -23,23 +62,25 @@
     return jnp.where(i % 2 == 1, (i + 1) // 2, (NZ - i // 2) % NZ)
 
 
-def kernel(vis_ref, q_ref, k_ref, v_ref, o_ref, qbuf, kv, relay, vx, obuf, acc, peak,
+def kernel(vis_ref, q_ref, k_ref, v_ref, o_ref, qbuf, kv, relay, cross, vx, obuf, acc, peak,
            s_a, s_b, p_a, p_b,
-           kv0_sem, q_sem, kv_sem, rl_sem, o_sem, in_send, f1_send, f2_send, f3_send, f4_send,
-           m_send, mr_send, o_send):
+           kv0_sem, q_sem, kv_sem, rl_sem, cross_sem, o_sem, in_send, f1_send, f2_send, f3_send, f4_send,
+           m_send, mr_send, cross_send, o_send):
     s = lax.axis_index("seq")
     h = lax.axis_index("head")
     z, xh = h // 2, h % 2
     core, chip = s % 2, s // 2
     xl, y = chip // 8, chip % 8
-    relay_to = (xl * 8 + (y + 6) % 8) * 2 + core
-    relay_chip = xl * 8 + (y + 2) % 8
-    relay_from = relay_chip * 2 + core
-    relays = relay_chip < 12
+
+    def relay_of(c):
+        return jnp.where((c >= 4) & (c < 8), c + 6, (c // 8) * 8 + (c % 8 + 6) % 8)
+
+    relay_to = relay_of(chip) * 2 + core
+    relays = (xl == 1) | (y >= 6) | (y <= 1)
+    relay_from = jnp.where((y >= 2) & (y <= 5), y + 2, xl * 8 + (y + 2) % 8) * 2 + core
     relay_dst = relay_from + 8
-    src8 = s - 8
-    chip8 = src8 // 2
-    relay_src = ((chip8 // 8) * 8 + (chip8 % 8 + 6) % 8) * 2 + core
+    relay_src = relay_of(chip - 4) * 2 + core
+    sends_cross, is_cross, gets_cross = chip == 7, chip == 15, chip == 8
 
     bar = pltpu.get_barrier_semaphore()
 
@@ -53,6 +94,7 @@
         (s + 4 < 32, s + 4), (s >= 4, s - 4),
         (s + 8 < 32, relay_to), (relays, relay_from),
         (relays, relay_dst), (s >= 8, relay_src),
+        (sends_cross, 30 + core), (is_cross, 14 + core), (is_cross, 16 + core), (gets_cross, 30 + core),
     ]
     count = 15
     for cond, other in links:
@@ -84,12 +126,19 @@
         pltpu.make_async_copy(src, dst, sem).start()
     for src, dst, _, sem in q_pieces(h):
         pltpu.make_async_copy(src, dst, sem).start()
-    for each in (pieces, q_pieces):
-        @pl.loop(1, 16)
-        def _(n):
-            p = ((z + offset(n // 2)) % NZ) * 2 + (xh + n) % 2
-            for src, dst, send, recv in each(p):
-                pltpu.make_async_remote_copy(src, dst, send, recv, device_id={"head": p}, device_id_type=MESH).start()
+
+    def spread(i, each):
+        for n in range(2):
+            p = ((z + offset(i)) % NZ) * 2 + (xh + n) % 2
+
+            @pl.when(p != h)
+            def _():
+                for src, dst, send, recv in each(p):
+                    pltpu.make_async_remote_copy(
+                        src, dst, send, recv, device_id={"head": p}, device_id_type=MESH).start()
+
+    for i in range(AHEAD):
+        spread(i, pieces)
 
     def zof(i):
         return (z + offset(i)) % NZ
@@ -103,6 +152,10 @@
     def own(i):
         r = zof(i)
         wait_bytes(kv.at[0, r], kv0_sem.at[r])
+        if i + AHEAD < NZ:
+            spread(i + AHEAD, pieces)
+        else:
+            spread(i + AHEAD - NZ, q_pieces)
 
         @pl.when(core == 0)
         def _():
@@ -130,9 +183,21 @@
     def to_four(i):
         r = zof(i)
 
-        @pl.when((s >= 2) & (s + 2 < 32))
+        @pl.when((s >= 2) & (s + 2 < 32) & (chip != 7))
         def _():
             pass_on(kv.at[2, r], kv.at[3, r], f3_send, kv_sem.at[2, r], s + 2)
+
+        @pl.when(sends_cross)
+        def _():
+            pass_on(kv.at[2, r], cross.at[r], f3_send, cross_sem.at[r], 30 + core)
+
+    def crossed(i):
+        r = zof(i)
+
+        @pl.when(is_cross)
+        def _():
+            wait_bytes(cross.at[r], cross_sem.at[r])
+            pass_on(cross.at[r], kv.at[3, r], cross_send, kv_sem.at[2, r], 16 + core)
 
     def four_back(i):
         r = zof(i)
@@ -160,18 +225,17 @@
     for j in range(5):
         vx[j, :, D:] = jnp.ones((BLOCK, D), BF16)
 
-    for k in range(NZ):
-        own(k)
-        if k >= 2:
-            two_back(k - 2)
-        if k in (3, 5, 7):
-            relayed((k - 3) // 2)
-    two_back(6)
-    two_back(7)
-
-    @pl.loop(0, NZ)
-    def _(i):
-        to_four(i)
+    for step, i in PLAN:
+        if step == "own":
+            own(i)
+        elif step == "two":
+            two_back(i)
+        elif step == "four":
+            to_four(i)
+        elif step == "relay":
+            relayed(i)
+        else:
+            crossed(i)
 
     @pl.when(s >= 1)
     def _():
@@ -186,9 +250,7 @@
     dims = (((1,), (1,)), ((), ()))
 
     def scores3(i, buf):
-        r = zof(i)
-        wait_bytes(qbuf.at[r], q_sem.at[r])
-        q = qbuf[r].reshape(2 * RUN, D)
+        q = qbuf[zof(i)].reshape(2 * RUN, D)
         for j in range(3):
             buf[:, j * BLOCK:(j + 1) * BLOCK] = lax.dot_general(
                 q, kv[j, :, 0].reshape(BLOCK, D), dims, preferred_element_type=F32)
@@ -215,18 +277,40 @@
     def value3(i, out):
         acc[zof(i)] = jnp.dot(out[...], vx[0:3].reshape(3 * BLOCK, 2 * D), preferred_element_type=F32)
 
+    def query(i):
+        r = zof(i)
+        wait_bytes(qbuf.at[r], q_sem.at[r])
+
+        @pl.when(i + AHEAD < NZ)
+        def _():
+            spread(i + AHEAD, q_pieces)
+
+    def events(at):
+        for step, k in LATER[at]:
+            {"relay": relayed, "cross": crossed, "old": four_back}[step](k)
+
+    query(0)
     scores3(0, s_a)
+    query(1)
     scores3(1, s_b)
     soft3(0, s_a, p_a)
 
     @pl.loop(0, 3)
     def _(n):
         i = 2 * n
-
-        relayed_if(relayed, n + 3)
+        for at in range(3):
+            @pl.when(n == at)
+            def _():
+                events(2 * at)
+        query(i + 2)
         value3(i, p_a)
         scores3(i + 2, s_a)
         soft3(i + 1, s_b, p_b)
+        for at in range(3):
+            @pl.when(n == at)
+            def _():
+                events(2 * at + 1)
+        query(i + 3)
         value3(i + 1, p_b)
         scores3(i + 3, s_b)
         soft3(i + 2, s_a, p_a)
@@ -234,11 +318,7 @@
     value3(6, p_a)
     soft3(7, s_b, p_b)
     value3(7, p_b)
-
-    @pl.loop(0, NZ)
-    def _(i):
-        four_back(i)
-
+    events(6)
     def scores1(j, i, buf):
         buf[:, :BLOCK] = lax.dot_general(
             qbuf[zof(i)].reshape(2 * RUN, D), kv[j, :, 0].reshape(BLOCK, D), dims, preferred_element_type=F32)
@@ -315,31 +395,27 @@
         ((s >= 4) & (s + 4 < 32), kv.at[0, 0:NZ - NM], f4_send),
         (s + 8 < 32, kv.at[0, 0:NM], m_send),
         (relays, kv.at[0, 0:NM], mr_send),
+        (is_cross, whole, cross_send),
     ):
         @pl.when(cond)
         def _():
             wait_bytes(ref, sem)
     wait_bytes(o_ref.at[:, :30 * D], o_send)
     wait_bytes(o_ref, o_sem)
-
-
-def relayed_if(relayed, i):
-    @pl.when(i < NM)
-    def _():
-        relayed(i)
 
 
 def body(queries, keys, values, visible):
     dma = pltpu.SemaphoreType.DMA
     return pl.pallas_call(
         kernel,
-        out_shape=jax.ShapeDtypeStruct(queries.shape, BF16),
+        out_shape=pltpu.VMEM(queries.shape, BF16),
         in_specs=[pl.BlockSpec(memory_space=pltpu.SMEM)] + [pl.BlockSpec(memory_space=pl.ANY)] * 3,
-        out_specs=pl.BlockSpec(memory_space=pl.ANY),
+        out_specs=pl.BlockSpec(memory_space=pltpu.VMEM),
         scratch_shapes=[
             pltpu.VMEM((NZ, 2, RUN, D), BF16),
             pltpu.VMEM((5, NZ, 2, RUN, D), BF16),
             pltpu.VMEM((NM, 2, RUN, D), BF16),
+            pltpu.VMEM((NZ, 2, RUN, D), BF16),
             pltpu.VMEM((5, BLOCK, 2 * D), BF16),
             pltpu.VMEM((NZ, RUN, 2 * D), BF16),
             pltpu.VMEM((NZ, 2 * RUN, 2 * D), F32),
@@ -348,8 +424,8 @@
             pltpu.VMEM((2 * RUN, 3 * BLOCK), F32),
             pltpu.VMEM((2 * RUN, 3 * BLOCK), BF16),
             pltpu.VMEM((2 * RUN, 3 * BLOCK), BF16),
-            dma((NZ,)), dma((NZ,)), dma((4, NZ)), dma((NM,)), dma,
-            dma((3,)), dma, dma, dma, dma, dma, dma, dma,
+            dma((NZ,)), dma((NZ,)), dma((4, NZ)), dma((NM,)), dma((NZ,)), dma,
+            dma((3,)), dma, dma, dma, dma, dma, dma, dma, dma,
         ],
         compiler_params=pltpu.CompilerParams(
             collective_id=0, has_side_effects=True, vmem_limit_bytes=56 * 2**20),

time: 82.3 us -> 73.3 us (0.89)
  Pallas kernels: 80.3 us -> 72.2 us
  local copies, waits for them, and re-layouts: 1.87 us -> 0.8 us
    pallas_call x1, Pallas kernels: 80.3 us -> 72.2 us  [body(): pl.pallas_call(kernel, out_shape=pltpu.VMEM(queries.shape, BF16), in_spec...]
    unnamed x1, local copies, waits for them, and re-layouts: 1.87 us -> 0.8 us
where the time goes in v2:
time: 73.3 us; the launch traced here: 73 us
  Pallas kernels  72.2 us (98%)
  local copies, waits for them, and re-layouts  0.8 us (1%)
    pallas_call x1, Pallas kernels, body(): pl.pallas_call(kernel, out_shape=pltpu.VMEM(queries.shape, BF16), in_spec...  72.2 us

profile of v2, /device:TPU:6, one launch (start us, length us, event | category | flops | bytes accessed | tf_op | source)
XLA Modules:
  0.0 73.0 jit_solution(6850360687133499645)
XLA Ops:
  0.0 72.2 %shard_map.46 = bf16[64,4096]{1,0:T(8,128)(2,1)S(1)} custom-call(s32[1,4]{1,0:T(1,128)} %vis_ref.1, bf16[64,4096]{1,0:T(8,128)(2,1)} %q_ref.1, bf16[64,2048]{1,0:T(8,128)(2,1)} %k_ref.1, bf16[64,2048]{1,0:T(8,128)(2,1)} %v_ref.1), custom_call_target="tpu_custom_call" | custom-call | flops 5000000000 | bytes 2000000 | tf_op jit(solution)/shard_map/pallas_call | solution.py:409
  72.2 0.8 %copy.6 = bf16[64,4096]{1,0:T(8,128)(2,1)} copy(bf16[64,4096]{1,0:T(8,128)(2,1)S(1)} %shard_map.46) | data formatting | bytes 1048576

commit v3 on v2

--- a/solution.py
+++ b/solution.py
@@ -13,45 +13,46 @@
 BLOCK = 1024
 SCALE2 = 168.0 ** (-0.5) * 1.4426950408889634
 AHEAD = 8
-NM = 5
+DOWN = (0, 1, 5, 6, 7)
+NM = len(DOWN)
 HIDE = 1e30
 PLAN = (
     ("own", 0),
     ("own", 1),
     ("own", 2),
     ("two", 0),
-    ("four", 0),
     ("relay", 0),
     ("own", 3),
     ("own", 4),
     ("two", 1),
-    ("four", 1),
+    ("relay", 1),
     ("two", 2),
-    ("four", 2),
-    ("relay", 1),
     ("own", 5),
     ("two", 3),
-    ("four", 3),
     ("own", 6),
     ("two", 4),
+    ("own", 7),
+    ("four", 0),
+    ("four", 1),
+    ("four", 2),
+    ("four", 3),
     ("four", 4),
-    ("own", 7),
     ("two", 5),
     ("four", 5),
-    ("relay", 2),
     ("two", 6),
     ("four", 6),
+    ("relay", 5),
     ("two", 7),
     ("four", 7),
 )
 LATER = (
-    (("cross", 0),),
-    (("cross", 1), ("relay", 3)),
-    (("cross", 2), ("cross", 3)),
-    (("cross", 4), ("relay", 4)),
-    (("cross", 5), ("old", 0), ("old", 1), ("old", 2), ("old", 3), ("old", 4), ("old", 5)),
-    (("cross", 6), ("old", 6)),
-    (("cross", 7), ("old", 7)),
+    (("cross", 0), ("old", 0), ),
+    (("cross", 1), ("old", 1), ("relay", 6), ),
+    (("cross", 2), ("old", 2), ),
+    (("cross", 3), ("old", 3), ("relay", 7), ),
+    (("cross", 4), ("old", 4), ),
+    (("cross", 5), ("old", 5), ),
+    (("cross", 6), ("old", 6), ("cross", 7), ("old", 7), ),
 )
 MESH = pl.DeviceIdType.MESH
 F32 = jnp.float32
@@ -165,9 +166,12 @@
         def _():
             pass_on(kv.at[0, r], kv.at[2, r], f2_send, kv_sem.at[1, r], s + 2)
 
-        @pl.when((s + 8 < 32) & (i < NM))
-        def _():
-            pass_on(kv.at[0, r], relay.at[i], m_send, rl_sem.at[i], relay_to)
+        if i in DOWN:
+            n = DOWN.index(i)
+
+            @pl.when(s + 8 < 32)
+            def _():
+                pass_on(kv.at[0, r], relay.at[n], m_send, rl_sem.at[n], relay_to)
 
     def two_back(i):
         r = zof(i)
@@ -206,17 +210,19 @@
         def _():
             wait_bytes(kv.at[3, r], kv_sem.at[2, r])
 
-        @pl.when((s >= 4) & (s + 4 < 32) & (i >= NM))
-        def _():
-            pass_on(kv.at[3, r], kv.at[4, r], f4_send, kv_sem.at[3, r], s + 4)
+        if i not in DOWN:
+            @pl.when((s >= 4) & (s + 4 < 32))
+            def _():
+                pass_on(kv.at[3, r], kv.at[4, r], f4_send, kv_sem.at[3, r], s + 4)
 
     def relayed(i):
         r = zof(i)
+        n = DOWN.index(i)
 
         @pl.when(relays)
         def _():
-            wait_bytes(relay.at[i], rl_sem.at[i])
-            pass_on(relay.at[i], kv.at[4, r], mr_send, kv_sem.at[3, r], relay_dst)
+            wait_bytes(relay.at[n], rl_sem.at[n])
+            pass_on(relay.at[n], kv.at[4, r], mr_send, kv_sem.at[3, r], relay_dst)
 
     for j, dist in ((1, 1), (2, 2), (3, 4), (4, 8)):
         @pl.when(s < dist)

time: 73.3 us -> 72.3 us (0.986)
  Pallas kernels: 72.2 us -> 71 us
    pallas_call x1, Pallas kernels: 72.2 us -> 71 us  [body(): pl.pallas_call(kernel, out_shape=pltpu.VMEM(queries.shape, BF16), in_spec...]
where the time goes in v3:
time: 72.3 us; the launch traced here: 71.8 us
  Pallas kernels  71 us (98%)
  local copies, waits for them, and re-layouts  0.8 us (1%)
    pallas_call x1, Pallas kernels, body(): pl.pallas_call(kernel, out_shape=pltpu.VMEM(queries.shape, BF16), in_spec...  71 us

profile of v3, /device:TPU:6, one launch (start us, length us, event | category | flops | bytes accessed | tf_op | source)
XLA Modules:
  0.0 71.8 jit_solution(17926167543690307408)
XLA Ops:
  0.0 71.0 %shard_map.46 = bf16[64,4096]{1,0:T(8,128)(2,1)S(1)} custom-call(s32[1,4]{1,0:T(1,128)} %vis_ref.1, bf16[64,4096]{1,0:T(8,128)(2,1)} %q_ref.1, bf16[64,2048]{1,0:T(8,128)(2,1)} %k_ref.1, bf16[64,2048]{1,0:T(8,128)(2,1)} %v_ref.1), custom_call_target="tpu_custom_call" | custom-call | flops 5000000000 | bytes 2000000 | tf_op jit(solution)/shard_map/pallas_call | solution.py:415
  71.0 0.8 %copy.6 = bf16[64,4096]{1,0:T(8,128)(2,1)} copy(bf16[64,4096]{1,0:T(8,128)(2,1)S(1)} %shard_map.46) | data formatting | bytes 1048576

commit v4 on v3

--- a/solution.py
+++ b/solution.py
@@ -39,20 +39,23 @@
     ("four", 4),
     ("two", 5),
     ("four", 5),
+    ("cross", 0),
     ("two", 6),
     ("four", 6),
     ("relay", 5),
+    ("cross", 1),
     ("two", 7),
     ("four", 7),
+    ("cross", 2),
 )
 LATER = (
-    (("cross", 0), ("old", 0), ),
-    (("cross", 1), ("old", 1), ("relay", 6), ),
-    (("cross", 2), ("old", 2), ),
-    (("cross", 3), ("old", 3), ("relay", 7), ),
-    (("cross", 4), ("old", 4), ),
-    (("cross", 5), ("old", 5), ),
-    (("cross", 6), ("old", 6), ("cross", 7), ("old", 7), ),
+    (("cross", 3), ("old", 0), ),
+    (("cross", 4), ("old", 1), ("relay", 6), ),
+    (("cross", 5), ("old", 2), ),
+    (("cross", 6), ("old", 3), ("relay", 7), ),
+    (("cross", 7), ("old", 4), ),
+    (("old", 5), ),
+    (("old", 6), ("old", 7), ),
 )
 MESH = pl.DeviceIdType.MESH
 F32 = jnp.float32

time: 72.3 us -> 70.1 us (0.970)
  Pallas kernels: 71 us -> 69.2 us
    pallas_call x1, Pallas kernels: 71 us -> 69.2 us  [body(): pl.pallas_call(kernel, out_shape=pltpu.VMEM(queries.shape, BF16), in_spec...]
where the time goes in v4:
time: 70.1 us; the launch traced here: 70 us
  Pallas kernels  69.2 us (99%)
  local copies, waits for them, and re-layouts  0.8 us (1%)
    pallas_call x1, Pallas kernels, body(): pl.pallas_call(kernel, out_shape=pltpu.VMEM(queries.shape, BF16), in_spec...  69.2 us

profile of v4, /device:TPU:6, one launch (start us, length us, event | category | flops | bytes accessed | tf_op | source)
XLA Modules:
  0.0 70.0 jit_solution(13277962777249949637)
XLA Ops:
  0.0 69.2 %shard_map.46 = bf16[64,4096]{1,0:T(8,128)(2,1)S(1)} custom-call(s32[1,4]{1,0:T(1,128)} %vis_ref.1, bf16[64,4096]{1,0:T(8,128)(2,1)} %q_ref.1, bf16[64,2048]{1,0:T(8,128)(2,1)} %k_ref.1, bf16[64,2048]{1,0:T(8,128)(2,1)} %v_ref.1), custom_call_target="tpu_custom_call" | custom-call | flops 5000000000 | bytes 2000000 | tf_op jit(solution)/shard_map/pallas_call | solution.py:418
  69.2 0.8 %copy.6 = bf16[64,4096]{1,0:T(8,128)(2,1)} copy(bf16[64,4096]{1,0:T(8,128)(2,1)S(1)} %shard_map.46) | data formatting | bytes 1048576
